TPU v7x, 32 devices: a whole 2x2x4 slice. The times are simulated.
32 devices in a mesh: dom: 8 (over z, y), band: 4 (over x, core).
Axes of the slice: x: 2, y: 2, z: 4, core: 2. Of those that a mesh axis runs over, the one named last changes fastest.
Arguments:
- orbitals: float32 [8, 128, 24, 576], P('dom', 'band'), may hold values from -6 to 6
- potential: float32 [8, 24, 576], P('dom'), may hold values from 0 to 3
- density_in: float32 [8, 24, 576], P('dom', 'band'), may hold values from 0.3 to 3
- occupation: float32 [128], replicated, may hold values from 0.5 to 2
- position: int32 [8], replicated, may hold values from 0 to 7, each once
- mixing: int32 [2], replicated, may hold values from 1 to 8
- correlation_weight: int32 [6], replicated, may hold values from 1 to 15
Outputs:
- orbitals_out: float32 [8, 128, 24, 576], P('dom', None, 'band')
- density: float32 [8, 24, 576], P('dom', 'band')
- hartree: float32 [8, 8, 8, 6], P('dom', 'band')
Inputs may be any that keep to these rules, and one draw needn't show every extreme that they name: position is a permutation: every place along the chain holds exactly one domain.
All inputs are finite; a program needn't handle non-finite values.
Results may differ from a plain program's by a relative error of at most 0.0001.
Values sent between devices are 32-bit elements; how exact they have to be, the bound alone decides.
A program may use at most 64 MiB of HBM per device.

v0:
```python
import functools

import jax
import jax.numpy as jnp
import ml_dtypes
import numpy as np
from jax import lax
from jax.experimental import pallas as pl
from jax.experimental.pallas import tpu as pltpu
from jax.sharding import PartitionSpec as P

BUFFER = 6
COARSEN = 3
CG = 8
CZ = 6
ROWS = 8
CENTER = 5.25
HALF_WIDTH = 4.25
BLEND_TOTAL = 16.0
HIGHEST = lax.Precision.HIGHEST
MESH = pl.DeviceIdType.MESH
F32, BF16 = jnp.float32, jnp.bfloat16


def split_np(table):
    high = table.astype(ml_dtypes.bfloat16)
    return high, (table - high.astype(np.float64)).astype(ml_dtypes.bfloat16)


def tables(grid, dom_count, band_count):
    line = np.eye(grid, k=1) + np.eye(grid, k=-1)
    adjacency = np.kron(line, np.eye(grid)) + np.kron(np.eye(grid), line)
    along_y = np.zeros((grid, CG))
    along_y[np.arange(grid), np.arange(grid) // COARSEN] = 1.0
    along_z = np.zeros((grid, CZ))
    core = np.arange(CZ * COARSEN)
    along_z[core, core // COARSEN] = 1.0
    coarsen = np.kron(along_y, along_z)
    order = np.arange(CG)
    cosine = np.sqrt(2.0 / CG) * np.cos(np.pi * order[:, None] * (order[None, :] + 0.5) / CG)
    cosine[0] *= np.sqrt(0.5)
    chain = dom_count * CZ
    place = np.arange(chain)
    sine = np.sqrt(2.0 / (chain + 1)) * np.sin(
        np.pi * (place[:, None] + 1.0) * (place[None, :] + 1.0) / (chain + 1)
    )
    spectral = np.einsum("ky,pzq->pyzkq", cosine, sine.reshape(dom_count, CZ, chain)).reshape(
        dom_count * CG * CZ, CG * chain
    )
    planes = grid // band_count
    coarse_x = planes // COARSEN
    forward = np.zeros((CG, band_count, ROWS))
    backward = np.zeros((band_count, ROWS, CG))
    for band in range(band_count):
        for plane in range(planes):
            forward[:, band, plane] = cosine[:, band * coarse_x + plane // COARSEN] / COARSEN**3
        for cell in range(coarse_x):
            backward[band, cell] = cosine[:, band * coarse_x + cell]
    side = 4.0 * np.sin(0.5 * np.pi * order / CG) ** 2
    depth = 4.0 * np.sin(0.5 * np.pi * (place + 1.0) / (chain + 1.0)) ** 2
    eigen = side[:, None, None] + side[None, :, None] + depth[None, None, :]
    inverse = (8.0 / chain**2 / eigen).reshape(CG, CG * chain)
    spectral_high, spectral_low = split_np(spectral)
    return (
        adjacency.astype(ml_dtypes.bfloat16),
        coarsen.astype(ml_dtypes.bfloat16),
        spectral_high,
        spectral_low,
        forward.reshape(CG, band_count * ROWS).astype(np.float32),
        backward.reshape(band_count * ROWS, CG).astype(np.float32),
        inverse.astype(np.float32),
    )


def split(values):
    high = values.astype(BF16)
    return high, (values - high.astype(F32)).astype(BF16)


def dot(a, b, precision=None):
    return jnp.dot(a, b, preferred_element_type=F32, precision=precision)


def dot_nt(a, b):
    return lax.dot_general(a, b, (((1,), (1,)), ((), ())), preferred_element_type=F32)


def kernel(
    sizes,
    orb_ref, pot_ref, din_ref, occ_ref, pos_ref, mix_ref, cw_ref,
    adj_ref, coarsen_ref, sph_ref, spl_ref, fwd_ref, bwd_ref, inv_ref,
    out_ref, den_ref, har_ref,
    diag, filt, full, parts, raw_src, raw_in, din_src, din_all, fresh_src, fresh_all,
    spec_src, spec_all, own_h, own_l,
    a2a_send, a2a_recv, raw_send, raw_recv, din_send, din_recv, fr_send, fr_recv, sp_send, sp_recv,
):
    grid, cells, nb, local, planes, n_dom, n_band = sizes
    dom, band = lax.axis_index("dom"), lax.axis_index("band")
    shifts = [r for r in range(1, n_band)]
    shifts.sort(key=lambda r: r % 2)
    chunks = local // 8

    barrier = pltpu.get_barrier_semaphore()
    for r in range(1, n_band):
        pl.semaphore_signal(barrier, inc=1, device_id={"band": lax.rem(band + r, n_band)}, device_id_type=MESH)
    for r in range(1, n_dom):
        pl.semaphore_signal(barrier, inc=1, device_id={"dom": lax.rem(dom + r, n_dom)}, device_id_type=MESH)

    for k in range(grid):
        row = (3.0 - CENTER + pot_ref[pl.ds(k, 1), :]) * (1.0 / HALF_WIDTH)
        diag[k] = jnp.broadcast_to(row, (8, cells))
    if planes < ROWS:
        din_src[...] = jnp.zeros_like(din_src)
        fresh_src[...] = jnp.zeros_like(fresh_src)
    din_src[pl.ds(0, planes), :] = din_ref[...]

    def neighbours(values):
        flat = values.reshape(grid * 8, cells)
        high, low = split(flat)
        both = dot(jnp.concatenate([high, low], 0), adj_ref[...])
        inside = (both[: grid * 8] + both[grid * 8 :]).reshape(grid, 8, cells)
        edge = jnp.zeros((1, 8, cells), F32)
        return (
            inside
            + jnp.concatenate([edge, values[:-1]], 0)
            + jnp.concatenate([values[1:], edge], 0)
        )

    def a2a_copy(r, c, start):
        peer = lax.rem(band + r, n_band)
        return pltpu.make_async_remote_copy(
            src_ref=filt.at[pl.ds(peer * planes, planes), pl.ds(start, 8), :],
            dst_ref=full.at[:, pl.ds(pl.multiple_of(band * local + start, 8), 8), :],
            send_sem=a2a_send.at[r - 1, c],
            recv_sem=a2a_recv.at[r - 1, c],
            device_id={"band": peer},
            device_id_type=MESH,
        )

    def filter_chunk(c):
        start = pl.multiple_of(c * 8, 8)
        first = orb_ref[:, pl.ds(start, 8), :]
        once = diag[...] * first - (0.5 / HALF_WIDTH) * neighbours(first)
        twice = 2.0 * (diag[...] * once - (0.5 / HALF_WIDTH) * neighbours(once)) - first
        filt[:, pl.ds(start, 8), :] = twice

    def send_chunk(c):
        start = pl.multiple_of(c * 8, 8)
        for r in shifts:
            a2a_copy(r, c, start).start()
        full[:, pl.ds(pl.multiple_of(band * local + start, 8), 8), :] = filt[
            pl.ds(band * planes, planes), pl.ds(start, 8), :
        ]

    filter_chunk(0)
    pl.semaphore_wait(barrier, n_band + n_dom - 2)
    send_chunk(0)

    def step(c, carry):
        filter_chunk(c)
        send_chunk(c)
        return carry

    lax.fori_loop(1, chunks, step, 0)

    def dom_copy(src, dst, send, recv, r):
        return pltpu.make_async_remote_copy(
            src_ref=src, dst_ref=dst.at[dom], send_sem=send.at[r - 1], recv_sem=recv.at[r - 1],
            device_id={"dom": lax.rem(dom + r, n_dom)}, device_id_type=MESH,
        )

    def band_copy(src, dst, send, recv, r):
        return pltpu.make_async_remote_copy(
            src_ref=src, dst_ref=dst.at[band], send_sem=send.at[r - 1], recv_sem=recv.at[r - 1],
            device_id={"band": lax.rem(band + r, n_band)}, device_id_type=MESH,
        )

    din_copies = [dom_copy(din_src, din_all, din_send, din_recv, r) for r in range(1, n_dom)]
    for copy in din_copies:
        copy.start()
    din_all[dom] = din_src[...]

    places = [pos_ref[d] for d in range(n_dom)]
    own_place = jnp.int32(0)
    for d in range(n_dom):
        own_place = own_place + jnp.where(dom == d, places[d], 0)
    block = CG * CZ
    total_h = jnp.zeros(own_h.shape, F32)
    total_l = jnp.zeros(own_l.shape, F32)
    for p in range(n_dom):
        pick = jnp.where(own_place == p, 1.0, 0.0).astype(F32)
        total_h = total_h + pick * sph_ref[pl.ds(p * block, block), :].astype(F32)
        total_l = total_l + pick * spl_ref[pl.ds(p * block, block), :].astype(F32)
    own_h[...] = total_h.astype(BF16)
    own_l[...] = total_l.astype(BF16)
    z = lax.rem(lax.broadcasted_iota(jnp.int32, (1, cells), 1), grid)
    weight = jnp.zeros((1, cells), F32)
    for j in range(BUFFER):
        value = cw_ref[j].astype(F32)
        weight = weight + jnp.where((z == j) | (z == grid - BUFFER + j), value, 0.0)
    row_id = lax.broadcasted_iota(jnp.int32, (nb, nb), 0)
    col_id = lax.broadcasted_iota(jnp.int32, (nb, nb), 1)
    eye = jnp.where(row_id == col_id, 1.0, 0.0).astype(F32)
    occupation = jnp.sum(eye * occ_ref[...], axis=1, keepdims=True)

    def wait_chunk(c, carry):
        start = pl.multiple_of(c * 8, 8)
        for r in shifts:
            a2a_copy(r, c, start).wait()
        return carry

    lax.fori_loop(0, chunks, wait_chunk, 0)

    product = jnp.zeros((nb, 2 * nb), F32)
    for k in range(planes):
        high, low = split(full[k])
        parts[k, pl.ds(0, nb), :] = high
        parts[k, pl.ds(nb, nb), :] = low
        product = product + dot_nt(high, parts[k])
    cross = product[:, nb:]
    raw_src[...] = product[:, :nb] + cross + cross.T
    raw_copies = [band_copy(raw_src, raw_in, raw_send, raw_recv, r) for r in shifts]
    for copy in raw_copies:
        copy.start()
    raw_in[band] = raw_src[...]
    for copy in raw_copies:
        copy.wait()
    raw = raw_in[0]
    for b in range(1, n_band):
        raw = raw + raw_in[b]
    norm = jnp.sqrt(jnp.sum(raw * raw, keepdims=True))
    scaling = jnp.sqrt(float(grid**3) / norm)
    gram = raw / norm
    linear = 1.5 * eye - 0.5 * gram
    cubic = dot(dot(linear, gram, HIGHEST), dot(linear, linear, HIGHEST), HIGHEST)
    poly = scaling * (1.5 * linear - 0.5 * cubic)
    poly_high, poly_low = split(poly)
    poly_twice = jnp.concatenate([poly_high, poly_high], 1)
    for k in range(planes):
        result = dot(poly_twice, parts[k]) + dot(poly_low, parts[k, pl.ds(0, nb), :])
        out_ref[k] = result
        fresh_src[pl.ds(k, 1), :] = jnp.sum(occupation * (result * result), axis=0, keepdims=True) * (1.0 / nb)

    fresh_copies = [dom_copy(fresh_src, fresh_all, fr_send, fr_recv, r) for r in range(1, n_dom)]
    for copy in fresh_copies:
        copy.start()
    fresh_all[dom] = fresh_src[...]
    for copy in din_copies:
        copy.wait()

    def ordered(ref):
        rows = []
        for p in range(n_dom):
            total = jnp.zeros((ROWS, cells), F32)
            for d in range(n_dom):
                total = total + jnp.where(places[d] == p, 1.0, 0.0).astype(F32) * ref[d]
            rows.append(total)
        return rows

    inflow = ordered(din_all)
    for copy in fresh_copies:
        copy.wait()
    fresh = ordered(fresh_all)

    gap = grid - BUFFER
    mix_new = jnp.full((1, cells), mix_ref[0].astype(F32))
    mix_old = jnp.full((1, cells), mix_ref[1].astype(F32))
    mixed = []
    own_density = jnp.zeros((ROWS, cells), F32)
    for p in range(n_dom):
        own = fresh[p]
        blended = own
        if p > 0:
            left = jnp.concatenate([fresh[p - 1][:, gap:], fresh[p - 1][:, :gap]], 1)
            low = (weight * left + (BLEND_TOTAL - weight) * own) / BLEND_TOTAL
            blended = jnp.where(z < BUFFER, low, blended)
        if p < n_dom - 1:
            right = jnp.concatenate([fresh[p + 1][:, cells - gap :], fresh[p + 1][:, : cells - gap]], 1)
            high = (weight * own + (BLEND_TOTAL - weight) * right) / BLEND_TOTAL
            blended = jnp.where(z >= gap, high, blended)
        value = (mix_new * blended + mix_old * inflow[p]) / (mix_new + mix_old)
        mixed.append(value)
        own_density = own_density + jnp.where(own_place == p, 1.0, 0.0).astype(F32) * value
    den_ref[...] = own_density[:planes]

    stacked = jnp.concatenate(mixed, 0)
    height = n_dom * ROWS
    high, low = split(stacked)
    both = dot(jnp.concatenate([high, low], 0), coarsen_ref[...])
    coarse = both[:height] + both[height:]
    wide = jnp.concatenate([coarse[p * ROWS : (p + 1) * ROWS] for p in range(n_dom)], 1)
    high, low = split(wide)
    spec_src[...] = dot(high, sph_ref[...]) + dot(low, sph_ref[...]) + dot(high, spl_ref[...])
    spec_copies = [band_copy(spec_src, spec_all, sp_send, sp_recv, r) for r in shifts]
    for copy in spec_copies:
        copy.start()
    spec_all[band] = spec_src[...]
    for copy in spec_copies:
        copy.wait()
    gathered = spec_all[...].reshape(n_band * ROWS, spec_src.shape[1])
    spectrum = dot(fwd_ref[...], gathered, HIGHEST) * inv_ref[...]
    mine = dot(bwd_ref[pl.ds(pl.multiple_of(band * ROWS, ROWS), ROWS), :], spectrum, HIGHEST)
    high, low = split(mine)
    field = dot_nt(high, own_h[...]) + dot_nt(low, own_h[...]) + dot_nt(high, own_l[...])
    har_ref[...] = field[: har_ref.shape[0]]


def body(orbitals, potential, density_in, occupation, position, mixing, correlation_weight):
    nb = occupation.shape[0]
    n_dom, n_band = lax.axis_size("dom"), lax.axis_size("band")
    _, local, grid, cells = orbitals.shape
    planes = density_in.shape[1]
    coarse_x = planes // COARSEN
    chain = CG * CZ * n_dom
    sizes = (grid, cells, nb, local, planes, n_dom, n_band)
    vmem = pl.BlockSpec(memory_space=pltpu.VMEM)
    smem = pl.BlockSpec(memory_space=pltpu.SMEM)
    consts = [jnp.asarray(t) for t in tables(grid, n_dom, n_band)]
    dma = pltpu.SemaphoreType.DMA
    chunks = local // 8
    out, density, hartree = pl.pallas_call(
        functools.partial(kernel, sizes),
        out_shape=(
            jax.ShapeDtypeStruct((planes, nb, cells), F32),
            jax.ShapeDtypeStruct((planes, cells), F32),
            jax.ShapeDtypeStruct((coarse_x, CG * CZ), F32),
        ),
        in_specs=[vmem] * 4 + [smem] * 3 + [vmem] * 7,
        out_specs=(vmem, vmem, vmem),
        scratch_shapes=[
            pltpu.VMEM((grid, 8, cells), F32),
            pltpu.VMEM((grid, local, cells), F32),
            pltpu.VMEM((planes, nb, cells), F32),
            pltpu.VMEM((planes, 2 * nb, cells), BF16),
            pltpu.VMEM((nb, nb), F32),
            pltpu.VMEM((n_band, nb, nb), F32),
            pltpu.VMEM((ROWS, cells), F32),
            pltpu.VMEM((n_dom, ROWS, cells), F32),
            pltpu.VMEM((ROWS, cells), F32),
            pltpu.VMEM((n_dom, ROWS, cells), F32),
            pltpu.VMEM((ROWS, chain), F32),
            pltpu.VMEM((n_band, ROWS, chain), F32),
            pltpu.VMEM((CG * CZ, chain), BF16),
            pltpu.VMEM((CG * CZ, chain), BF16),
            dma((n_band - 1, chunks)), dma((n_band - 1, chunks)),
            dma((n_band - 1,)), dma((n_band - 1,)),
            dma((n_dom - 1,)), dma((n_dom - 1,)),
            dma((n_dom - 1,)), dma((n_dom - 1,)),
            dma((n_band - 1,)), dma((n_band - 1,)),
        ],
        compiler_params=pltpu.CompilerParams(
            collective_id=0, has_side_effects=True, vmem_limit_bytes=56 * 1024 * 1024
        ),
    )(
        jnp.swapaxes(orbitals[0], 0, 1), potential[0], density_in[0], occupation.reshape(1, nb),
        position, mixing, correlation_weight, *consts,
    )
    return (
        jnp.swapaxes(out, 0, 1)[None],
        density[None],
        hartree.reshape(1, coarse_x, CG, CZ),
    )


def solution(mesh):
    return jax.shard_map(
        body,
        mesh=mesh,
        in_specs=(
            P("dom", "band", None, None),
            P("dom", None, None),
            P("dom", "band", None),
            P(),
            P(),
            P(),
            P(),
        ),
        out_specs=(
            P("dom", None, "band", None),
            P("dom", "band", None),
            P("dom", "band", None, None),
        ),
        check_vma=False,
    )
```

profile of v0, /device:TPU:0, one launch (start us, length us, event | category | flops | bytes accessed | tf_op | source)
XLA Modules:
  0.0 56.6 jit_solution(10563140176375814630)
XLA Ops:
  0.6 1.3 %copy.29 = f32[1,6,576]{2,1,0:T(8,128)} copy(f32[1,6,576]{2,0,1:T(1,128)} %param.16) | data formatting | bytes 27648
  2.0 3.2 %copy.28 = f32[1,32,24,576]{3,1,2,0:T(8,128)} copy(f32[1,32,24,576]{3,2,1,0:T(8,128)} %param.14) | data formatting | bytes 3538944 | tf_op args[0]
  5.2 47.2 %shard_map.157 = (f32[6,128,576]{2,1,0:T(8,128)}, f32[6,576]{1,0:T(8,128)}, f32[2,48]{1,0:T(2,128)}) custom-call(f32[24,32,576]{2,1,0:T(8,128)} %bitcast.14, f32[24,576]{1,0:T(8,128)} %bitcast.17, f32[6,576]{1,0:T(8,128)} %bitcast.16, f32[1,128]{1,0:T(1,128)} %bitcast.19, s32[8]{0:T(128)} %pos_ref.1, s32[2]{0:T(128)} %mix_ref.1, s32[6]{0:T(128)} %cw_ref.1, ...), custom_call_target="tpu_custom_call" | custom-call | tf_op jit(solution)/shard_map/pallas_call | solution.py:321
  52.4 0.0 copy-start
  52.4 0.0 copy-start.1
  52.5 2.8 %copy.22 = f32[1,128,6,576]{1,3,2,0:T(8,128)} copy(f32[1,128,6,576]{3,1,2,0:T(8,128)} %bitcast.15) | data formatting | bytes 3538944
  55.2 0.0 copy-done
  55.2 0.6 %copy.23 = f32[1,6,576]{2,0,1:T(1,128)} copy(f32[1,6,576]{2,1,0:T(8,128)S(1)} %bitcast.18) | data formatting | bytes 27648
  55.8 0.0 copy-done.1
  55.8 0.1 reshape.13
  55.9 0.7 %copy.24 = f32[1,2,8,6]{2,1,3,0:T(2,128)} copy(f32[1,2,8,6]{3,2,1,0:T(8,128)S(1)} %reshape.13) | data formatting | bytes 768
Async XLA Ops:
  52.4 2.8 %copy-start = (f32[6,576]{1,0:T(8,128)S(1)}, f32[6,576]{1,0:T(8,128)}, u32[]{:S(2)}) copy-start(f32[6,576]{1,0:T(8,128)} %get-tuple-element.7) | copy-start | bytes 41476
  52.4 3.4 %copy-start.1 = (f32[2,48]{1,0:T(2,128)S(1)}, f32[2,48]{1,0:T(2,128)}, u32[]{:S(2)}) copy-start(f32[2,48]{1,0:T(2,128)} %get-tuple-element.8) | copy-start | bytes 1156
where the time goes:
time: 56.9 us; the launch traced here: 56.6 us
  Pallas kernels  47.2 us (83%)
  local copies, waits for them, and re-layouts  8.7 us (15%)
  between operations  0.66 us (1%)
    pallas_call x1, Pallas kernels, body(): pl.pallas_call(functools.partial(kernel, sizes), out_shape=(jax.ShapeDtyp...  47.2 us
    unnamed x9, local copies, waits for them, and re-layouts  8.62 us

commit v1 on v0

--- a/solution.py
+++ b/solution.py
@@ -28,14 +28,12 @@
 
 
 def tables(grid, dom_count, band_count):
-    line = np.eye(grid, k=1) + np.eye(grid, k=-1)
-    adjacency = np.kron(line, np.eye(grid)) + np.kron(np.eye(grid), line)
     along_y = np.zeros((grid, CG))
     along_y[np.arange(grid), np.arange(grid) // COARSEN] = 1.0
     along_z = np.zeros((grid, CZ))
     core = np.arange(CZ * COARSEN)
     along_z[core, core // COARSEN] = 1.0
-    coarsen = np.kron(along_y, along_z)
+    coarsen = np.einsum("yY,zZ->yzZY", along_y, along_z).reshape(grid * grid, CZ * CG)
     order = np.arange(CG)
     cosine = np.sqrt(2.0 / CG) * np.cos(np.pi * order[:, None] * (order[None, :] + 0.5) / CG)
     cosine[0] *= np.sqrt(0.5)
@@ -44,7 +42,7 @@
     sine = np.sqrt(2.0 / (chain + 1)) * np.sin(
         np.pi * (place[:, None] + 1.0) * (place[None, :] + 1.0) / (chain + 1)
     )
-    spectral = np.einsum("ky,pzq->pyzkq", cosine, sine.reshape(dom_count, CZ, chain)).reshape(
+    spectral = np.einsum("ky,pzq->pzykq", cosine, sine.reshape(dom_count, CZ, chain)).reshape(
         dom_count * CG * CZ, CG * chain
     )
     planes = grid // band_count
@@ -62,7 +60,6 @@
     inverse = (8.0 / chain**2 / eigen).reshape(CG, CG * chain)
     spectral_high, spectral_low = split_np(spectral)
     return (
-        adjacency.astype(ml_dtypes.bfloat16),
         coarsen.astype(ml_dtypes.bfloat16),
         spectral_high,
         spectral_low,
@@ -88,13 +85,14 @@
 def kernel(
     sizes,
     orb_ref, pot_ref, din_ref, occ_ref, pos_ref, mix_ref, cw_ref,
-    adj_ref, coarsen_ref, sph_ref, spl_ref, fwd_ref, bwd_ref, inv_ref,
+    coarsen_ref, sph_ref, spl_ref, fwd_ref, bwd_ref, inv_ref,
     out_ref, den_ref, har_ref,
-    diag, filt, full, parts, raw_src, raw_in, din_src, din_all, fresh_src, fresh_all,
+    diag, before, once, filt, full, result, parts, raw_src, raw_in, din_src, din_all, fresh_src, fresh_all,
     spec_src, spec_all, own_h, own_l,
     a2a_send, a2a_recv, raw_send, raw_recv, din_send, din_recv, fr_send, fr_recv, sp_send, sp_recv,
 ):
-    grid, cells, nb, local, planes, n_dom, n_band = sizes
+    grid, cells, nb, local, planes, pack, n_dom, n_band = sizes
+    groups = planes // pack
     dom, band = lax.axis_index("dom"), lax.axis_index("band")
     shifts = [r for r in range(1, n_band)]
     shifts.sort(key=lambda r: r % 2)
@@ -106,30 +104,36 @@
     for r in range(1, n_dom):
         pl.semaphore_signal(barrier, inc=1, device_id={"dom": lax.rem(dom + r, n_dom)}, device_id_type=MESH)
 
+    wide_cells = diag.shape[2]
+    lane = lax.broadcasted_iota(jnp.int32, (8, wide_cells), 1)
+    depth = lax.rem(lane, grid)
+    inside = jnp.where(lane < cells, 1.0, 0.0).astype(F32)
+    above = jnp.where((lane < cells) & (depth > 0), 1.0, 0.0).astype(F32)
+    below = jnp.where((lane < cells) & (depth < grid - 1), 1.0, 0.0).astype(F32)
     for k in range(grid):
         row = (3.0 - CENTER + pot_ref[pl.ds(k, 1), :]) * (1.0 / HALF_WIDTH)
-        diag[k] = jnp.broadcast_to(row, (8, cells))
+        diag[k, :, pl.ds(0, cells)] = jnp.broadcast_to(row, (8, cells))
+        for ref in (diag, before):
+            ref[k, :, pl.ds(cells, wide_cells - cells)] = jnp.zeros((8, wide_cells - cells), F32)
     if planes < ROWS:
         din_src[...] = jnp.zeros_like(din_src)
         fresh_src[...] = jnp.zeros_like(fresh_src)
-    din_src[pl.ds(0, planes), :] = din_ref[...]
-
-    def neighbours(values):
-        flat = values.reshape(grid * 8, cells)
-        high, low = split(flat)
-        both = dot(jnp.concatenate([high, low], 0), adj_ref[...])
-        inside = (both[: grid * 8] + both[grid * 8 :]).reshape(grid, 8, cells)
-        edge = jnp.zeros((1, 8, cells), F32)
-        return (
-            inside
-            + jnp.concatenate([edge, values[:-1]], 0)
-            + jnp.concatenate([values[1:], edge], 0)
-        )
+    din_src[pl.ds(0, planes), :] = din_ref[:, 0, :]
+
+    def shifted(ref, k):
+        here = ref[k]
+        total = pltpu.roll(here, grid, 1) + pltpu.roll(here, wide_cells - grid, 1)
+        total = total + above * pltpu.roll(here, 1, 1) + below * pltpu.roll(here, wide_cells - 1, 1)
+        if k > 0:
+            total = total + ref[k - 1]
+        if k < grid - 1:
+            total = total + ref[k + 1]
+        return diag[k] * here - (0.5 / HALF_WIDTH) * total
 
     def a2a_copy(r, c, start):
         peer = lax.rem(band + r, n_band)
         return pltpu.make_async_remote_copy(
-            src_ref=filt.at[pl.ds(peer * planes, planes), pl.ds(start, 8), :],
+            src_ref=filt.at[pl.ds(peer * groups, groups), pl.ds(start, 8), :],
             dst_ref=full.at[:, pl.ds(pl.multiple_of(band * local + start, 8), 8), :],
             send_sem=a2a_send.at[r - 1, c],
             recv_sem=a2a_recv.at[r - 1, c],
@@ -139,17 +143,21 @@
 
     def filter_chunk(c):
         start = pl.multiple_of(c * 8, 8)
-        first = orb_ref[:, pl.ds(start, 8), :]
-        once = diag[...] * first - (0.5 / HALF_WIDTH) * neighbours(first)
-        twice = 2.0 * (diag[...] * once - (0.5 / HALF_WIDTH) * neighbours(once)) - first
-        filt[:, pl.ds(start, 8), :] = twice
+        before[:, :, pl.ds(0, cells)] = jnp.swapaxes(orb_ref[pl.ds(start, 8)], 0, 1)
+        for k in range(grid):
+            once[k] = inside * shifted(before, k)
+        for j in range(grid // pack):
+            pieces = [
+                (2.0 * shifted(once, k) - before[k])[:, :cells] for k in range(j * pack, (j + 1) * pack)
+            ]
+            filt[j, pl.ds(start, 8), :] = pieces[0] if pack == 1 else jnp.concatenate(pieces, 1)
 
     def send_chunk(c):
         start = pl.multiple_of(c * 8, 8)
         for r in shifts:
             a2a_copy(r, c, start).start()
         full[:, pl.ds(pl.multiple_of(band * local + start, 8), 8), :] = filt[
-            pl.ds(band * planes, planes), pl.ds(start, 8), :
+            pl.ds(band * groups, groups), pl.ds(start, 8), :
         ]
 
     filter_chunk(0)
@@ -212,7 +220,7 @@
     lax.fori_loop(0, chunks, wait_chunk, 0)
 
     product = jnp.zeros((nb, 2 * nb), F32)
-    for k in range(planes):
+    for k in range(groups):
         high, low = split(full[k])
         parts[k, pl.ds(0, nb), :] = high
         parts[k, pl.ds(nb, nb), :] = low
@@ -236,15 +244,19 @@
     poly = scaling * (1.5 * linear - 0.5 * cubic)
     poly_high, poly_low = split(poly)
     poly_twice = jnp.concatenate([poly_high, poly_high], 1)
-    for k in range(planes):
-        result = dot(poly_twice, parts[k]) + dot(poly_low, parts[k, pl.ds(0, nb), :])
-        out_ref[k] = result
-        fresh_src[pl.ds(k, 1), :] = jnp.sum(occupation * (result * result), axis=0, keepdims=True) * (1.0 / nb)
+    for j in range(groups):
+        rotated = dot(poly_twice, parts[j]) + dot(poly_low, parts[j, pl.ds(0, nb), :])
+        result[j] = rotated
+        row = jnp.sum(occupation * (rotated * rotated), axis=0, keepdims=True) * (1.0 / nb)
+        for i in range(pack):
+            fresh_src[pl.ds(j * pack + i, 1), :] = row[:, i * cells : (i + 1) * cells]
 
     fresh_copies = [dom_copy(fresh_src, fresh_all, fr_send, fr_recv, r) for r in range(1, n_dom)]
     for copy in fresh_copies:
         copy.start()
     fresh_all[dom] = fresh_src[...]
+    for j in range(groups):
+        out_ref[j] = result[j].T
     for copy in din_copies:
         copy.wait()
 
@@ -281,7 +293,7 @@
         value = (mix_new * blended + mix_old * inflow[p]) / (mix_new + mix_old)
         mixed.append(value)
         own_density = own_density + jnp.where(own_place == p, 1.0, 0.0).astype(F32) * value
-    den_ref[...] = own_density[:planes]
+    den_ref[:, 0, :] = own_density[:planes]
 
     stacked = jnp.concatenate(mixed, 0)
     height = n_dom * ROWS
@@ -302,7 +314,8 @@
     mine = dot(bwd_ref[pl.ds(pl.multiple_of(band * ROWS, ROWS), ROWS), :], spectrum, HIGHEST)
     high, low = split(mine)
     field = dot_nt(high, own_h[...]) + dot_nt(low, own_h[...]) + dot_nt(high, own_l[...])
-    har_ref[...] = field[: har_ref.shape[0]]
+    for cell in range(CZ):
+        har_ref[cell] = field[: har_ref.shape[1], cell * CG : (cell + 1) * CG]
 
 
 def body(orbitals, potential, density_in, occupation, position, mixing, correlation_weight):
@@ -312,7 +325,10 @@
     planes = density_in.shape[1]
     coarse_x = planes // COARSEN
     chain = CG * CZ * n_dom
-    sizes = (grid, cells, nb, local, planes, n_dom, n_band)
+    pack = 2 if planes % 2 == 0 else 1
+    groups = planes // pack
+    wide_cells = -(-(cells + grid) // 128) * 128
+    sizes = (grid, cells, nb, local, planes, pack, n_dom, n_band)
     vmem = pl.BlockSpec(memory_space=pltpu.VMEM)
     smem = pl.BlockSpec(memory_space=pltpu.SMEM)
     consts = [jnp.asarray(t) for t in tables(grid, n_dom, n_band)]
@@ -321,17 +337,20 @@
     out, density, hartree = pl.pallas_call(
         functools.partial(kernel, sizes),
         out_shape=(
-            jax.ShapeDtypeStruct((planes, nb, cells), F32),
-            jax.ShapeDtypeStruct((planes, cells), F32),
-            jax.ShapeDtypeStruct((coarse_x, CG * CZ), F32),
+            jax.ShapeDtypeStruct((groups, pack * cells, nb), F32),
+            jax.ShapeDtypeStruct((planes, 1, cells), F32),
+            jax.ShapeDtypeStruct((CZ, coarse_x, CG), F32),
         ),
-        in_specs=[vmem] * 4 + [smem] * 3 + [vmem] * 7,
+        in_specs=[vmem] * 4 + [smem] * 3 + [vmem] * 6,
         out_specs=(vmem, vmem, vmem),
         scratch_shapes=[
-            pltpu.VMEM((grid, 8, cells), F32),
-            pltpu.VMEM((grid, local, cells), F32),
-            pltpu.VMEM((planes, nb, cells), F32),
-            pltpu.VMEM((planes, 2 * nb, cells), BF16),
+            pltpu.VMEM((grid, 8, wide_cells), F32),
+            pltpu.VMEM((grid, 8, wide_cells), F32),
+            pltpu.VMEM((grid, 8, wide_cells), F32),
+            pltpu.VMEM((grid // pack, local, pack * cells), F32),
+            pltpu.VMEM((groups, nb, pack * cells), F32),
+            pltpu.VMEM((groups, nb, pack * cells), F32),
+            pltpu.VMEM((groups, 2 * nb, pack * cells), BF16),
             pltpu.VMEM((nb, nb), F32),
             pltpu.VMEM((n_band, nb, nb), F32),
             pltpu.VMEM((ROWS, cells), F32),
@@ -352,13 +371,13 @@
             collective_id=0, has_side_effects=True, vmem_limit_bytes=56 * 1024 * 1024
         ),
     )(
-        jnp.swapaxes(orbitals[0], 0, 1), potential[0], density_in[0], occupation.reshape(1, nb),
+        orbitals[0], potential[0], jnp.swapaxes(density_in, 0, 1), occupation.reshape(1, nb),
         position, mixing, correlation_weight, *consts,
     )
     return (
-        jnp.swapaxes(out, 0, 1)[None],
-        density[None],
-        hartree.reshape(1, coarse_x, CG, CZ),
+        jnp.transpose(out.reshape(planes, cells, nb), (2, 0, 1))[None],
+        jnp.swapaxes(density, 0, 1),
+        jnp.transpose(hartree, (1, 2, 0))[None],
     )
 
 

time: 56.9 us -> 50.3 us (0.88)
  local copies, waits for them, and re-layouts: 8.7 us -> 4.01 us
  Pallas kernels: 47.2 us -> 45.4 us
    unnamed x9 -> x7, local copies, waits for them, and re-layouts: 8.62 us -> 4.01 us
    pallas_call x1, Pallas kernels: 47.2 us -> 45.4 us  [body(): pl.pallas_call(functools.partial(kernel, sizes), out_shape=(jax.ShapeDtyp...]
where the time goes in v1:
time: 50.3 us; the launch traced here: 50.1 us
  Pallas kernels  45.4 us (90%)
  local copies, waits for them, and re-layouts  4.01 us (8%)
  between operations  0.66 us (1%)
    pallas_call x1, Pallas kernels, body(): pl.pallas_call(functools.partial(kernel, sizes), out_shape=(jax.ShapeDtyp...  45.4 us
    unnamed x7, local copies, waits for them, and re-layouts  4.01 us

profile of v1, /device:TPU:0, one launch (start us, length us, event | category | flops | bytes accessed | tf_op | source)
XLA Modules:
  0.0 50.1 jit_solution(4954919369655993263)
XLA Ops:
  0.6 45.4 %shard_map.148 = (f32[3,1152,128]{2,1,0:T(8,128)}, f32[6,1,576]{2,1,0:T(1,128)}, f32[6,2,8]{2,1,0:T(2,128)}) custom-call(f32[32,24,576]{2,1,0:T(8,128)} %bitcast.13, f32[24,576]{1,0:T(8,128)} %bitcast.15, f32[6,1,576]{2,1,0:T(1,128)} %bitcast.16, f32[1,128]{1,0:T(1,128)} %bitcast.19, s32[8]{0:T(128)} %pos_ref.1, s32[2]{0:T(128)} %mix_ref.1, s32[6]{0:T(128)} %cw_ref.1, ...), custom_call_target="tpu_custom_call" | custom-call | tf_op jit(solution)/shard_map/pallas_call | solution.py:337
  46.1 0.0 copy-start
  46.1 0.0 copy-start.1
  46.1 2.8 %copy.19 = f32[1,128,6,576]{1,3,2,0:T(8,128)} copy(f32[1,128,6,576]{1,3,2,0:T(8,128)} %bitcast.14) | data formatting | bytes 3538944
  48.9 0.0 copy-done
  48.9 0.6 %copy.20 = f32[1,6,576]{2,0,1:T(1,128)} copy(f32[1,6,576]{2,0,1:T(1,128)S(1)} %bitcast.17) | data formatting | bytes 27648
  49.5 0.0 copy-done.1
  49.5 0.6 %copy.21 = f32[1,2,8,6]{2,1,3,0:T(2,128)} copy(f32[1,2,8,6]{2,1,3,0:T(2,128)S(1)} %bitcast.18) | data formatting | bytes 768
Async XLA Ops:
  46.1 2.8 %copy-start = (f32[6,1,576]{2,1,0:T(1,128)S(1)}, f32[6,1,576]{2,1,0:T(1,128)}, u32[]{:S(2)}) copy-start(f32[6,1,576]{2,1,0:T(1,128)} %get-tuple-element.7) | copy-start | bytes 41476
  46.1 3.4 %copy-start.1 = (f32[6,2,8]{2,1,0:T(2,128)S(1)}, f32[6,2,8]{2,1,0:T(2,128)}, u32[]{:S(2)}) copy-start(f32[6,2,8]{2,1,0:T(2,128)} %get-tuple-element.8) | copy-start | bytes 1156

commit v2 on v1

--- a/solution.py
+++ b/solution.py
@@ -316,6 +316,17 @@
     field = dot_nt(high, own_h[...]) + dot_nt(low, own_h[...]) + dot_nt(high, own_l[...])
     for cell in range(CZ):
         har_ref[cell] = field[: har_ref.shape[1], cell * CG : (cell + 1) * CG]
+
+
+def hand_over(out_ref, den_ref, har_ref, out_last, den_last, har_last, sems):
+    pieces = out_ref.shape[0]
+    copies = [pltpu.make_async_copy(out_ref.at[k], out_last.at[k], sems.at[k]) for k in range(pieces)]
+    for copy in copies:
+        copy.start()
+    den_last[...] = den_ref[...]
+    har_last[...] = har_ref[...]
+    for copy in copies:
+        copy.wait()
 
 
 def body(orbitals, potential, density_in, occupation, position, mixing, correlation_weight):
@@ -374,8 +385,17 @@
         orbitals[0], potential[0], jnp.swapaxes(density_in, 0, 1), occupation.reshape(1, nb),
         position, mixing, correlation_weight, *consts,
     )
+    any_space = pl.BlockSpec(memory_space=pl.ANY)
+    out = out.reshape(planes, cells, nb)
+    out, density, hartree = pl.pallas_call(
+        hand_over,
+        out_shape=tuple(jax.ShapeDtypeStruct(a.shape, F32) for a in (out, density, hartree)),
+        in_specs=[any_space, vmem, vmem],
+        out_specs=(any_space, vmem, vmem),
+        scratch_shapes=[dma((planes,))],
+    )(out, density, hartree)
     return (
-        jnp.transpose(out.reshape(planes, cells, nb), (2, 0, 1))[None],
+        jnp.transpose(out, (2, 0, 1))[None],
         jnp.swapaxes(density, 0, 1),
         jnp.transpose(hartree, (1, 2, 0))[None],
     )

time: 50.3 us -> 102 us (2.03)
  Pallas kernels: 45.4 us -> 102 us
  local copies, waits for them, and re-layouts: 4.01 us -> 0 us
    pallas_call x0 -> x1, Pallas kernels: none -> 56.1 us  [body(): pl.pallas_call(hand_over, out_shape=tuple((jax.ShapeDtypeStruct(a.shape,...]
    unnamed x7 -> x0, local copies, waits for them, and re-layouts: 4.01 us -> none
where the time goes in v2:
time: 102 us
  Pallas kernels  102 us (100%)
    pallas_call x1, Pallas kernels, body(): pl.pallas_call(hand_over, out_shape=tuple((jax.ShapeDtypeStruct(a.shape,...  56.1 us
    pallas_call x1, Pallas kernels, body(): pl.pallas_call(functools.partial(kernel, sizes), out_shape=(jax.ShapeDtyp...  45.4 us

profile of v2, /device:TPU:0, one launch (start us, length us, event | category | flops | bytes accessed | tf_op | source)
XLA Modules:
  0.0 102.2 jit_solution(3454402541893578981)
XLA Ops:
  0.6 45.4 %shard_map.148 = (f32[3,1152,128]{2,1,0:T(8,128)}, f32[6,1,576]{2,1,0:T(1,128)}, f32[6,2,8]{2,1,0:T(2,128)}) custom-call(f32[32,24,576]{2,1,0:T(8,128)} %bitcast.12, f32[24,576]{1,0:T(8,128)} %bitcast.14, f32[6,1,576]{2,1,0:T(1,128)} %bitcast.15, f32[1,128]{1,0:T(1,128)} %bitcast.16, s32[8]{0:T(128)} %pos_ref.1, s32[2]{0:T(128)} %mix_ref.1, s32[6]{0:T(128)} %cw_ref.1, ...), custom_call_target="tpu_custom_call" | custom-call | tf_op jit(solution)/shard_map/pallas_call | solution.py:348
  46.1 56.1 %shard_map.149 = (f32[6,576,128]{2,1,0:T(8,128)}, f32[6,1,576]{2,1,0:T(1,128)}, f32[6,2,8]{2,1,0:T(2,128)}) custom-call(f32[6,576,128]{2,1,0:T(8,128)} %bitcast.13, f32[6,1,576]{2,1,0:T(1,128)} %get-tuple-element.10.den_ref, f32[6,2,8]{2,1,0:T(2,128)} %get-tuple-element.11.har_ref), custom_call_target="tpu_custom_call" | custom-call | tf_op jit(solution)/shard_map/pallas_call | solution.py:390
